TPU v7x, 32 devices: a whole 2x2x4 slice. The times are simulated.
32 devices in a mesh: frames: 8 (over z, x), blocks: 4 (over y, core).
Axes of the slice: x: 2, y: 2, z: 4, core: 2. Of those that a mesh axis runs over, the one named last changes fastest.
Arguments:
- frames_data: bfloat16 [28672, 2048], P('frames', 'blocks'), may hold values from -8 to 14
- traj_ids: int32 [28672], P('frames'), may hold values from 0 to 63, never falling along the last dimension, each value on 1 to 7168 neighbouring positions
Outputs:
- cov_zero: float32 [2048, 2048], P('frames', 'blocks')
- cov_lag: float32 [2048, 2048], P('frames', 'blocks')
Inputs may be any that keep to these rules, and one draw needn't show every extreme that they name: `traj_ids`: ids never fall along the frames; each trajectory is a contiguous run of 1 to 7168 frames and some trajectory has exactly 7168.
All inputs are finite; a program needn't handle non-finite values.
Results may differ from a plain program's by a relative error of at most 0.0003.
Values may be sent and summed in bfloat16 or wider, within the bound.
A program may use at most 64 MiB of HBM per device.

v0:
```python
import jax
import jax.numpy as jnp
from jax import lax
from jax.sharding import PartitionSpec as P

LAG = 64


def shifted(value, axis, steps):
    count = lax.axis_size(axis)
    first, last = (max(0, -steps), min(count, count - steps))
    return lax.ppermute(value, axis, [(source, source + steps) for source in range(first, last)])


def shards(frames_data, traj_ids):
    own_cols = frames_data.shape[1]
    marks = traj_ids + 1
    rim_marks = shifted(marks[:LAG], "frames", -1)
    rim_feats = shifted(frames_data[:LAG], "frames", -1)
    ahead = jnp.concatenate([marks[LAG:], rim_marks])
    valid = ahead == marks
    zeros = jnp.zeros_like(frames_data)
    current = jnp.where(valid[:, None], frames_data, zeros)
    later = jnp.concatenate([frames_data[LAG:], rim_feats], axis=0)
    count_local = jnp.sum(valid.astype(jnp.float32))
    sums_zero = jnp.sum(current.astype(jnp.float32), axis=0)
    sums_lag = jnp.sum(jnp.where(valid[:, None], later, zeros).astype(jnp.float32), axis=0)
    both_own = jnp.concatenate([current, later], axis=1)
    terms = lax.dot_general(
        lax.all_gather(current, "blocks", axis=1, tiled=True),
        both_own,
        (((0,), (0,)), ((), ())),
        preferred_element_type=jnp.float32,
    )
    reduced = lax.psum_scatter(terms, "frames", scatter_dimension=0, tiled=True)
    plain = reduced[:, :own_cols]
    lagged = reduced[:, own_cols:]
    row_count = plain.shape[0]
    row_start = lax.axis_index("frames") * row_count
    total_zero, total_lag, count = lax.psum((sums_zero, sums_lag, count_local), "frames")
    mean_cols = total_zero / count
    lag_cols = total_lag / count
    mean_all = lax.all_gather(mean_cols, "blocks", axis=0, tiled=True)
    mean_rows = lax.dynamic_slice_in_dim(mean_all, row_start, row_count, 0)
    cov_zero = plain / count - mean_rows[:, None] * mean_cols[None, :]
    cov_lag = lagged / count - mean_rows[:, None] * lag_cols[None, :]
    return (cov_zero, cov_lag)


def solution(mesh):
    return jax.shard_map(
        shards,
        mesh=mesh,
        in_specs=(P("frames", "blocks"), P("frames")),
        out_specs=(P("frames", "blocks"), P("frames", "blocks")),
        check_vma=False,
    )
```

profile of v0, /device:TPU:26, one launch (start us, length us, event | category | flops | bytes accessed | tf_op | source)
XLA Modules:
  0.0 297.6 jit_solution(6158074217739325567)
XLA Ops:
  7.2 0.0 all-gather.3.cloned.1.call-start
  7.2 0.0 copy-start
  7.2 0.9 broadcast_add_fusion
  8.1 2.6 collective-permute-start
  10.7 0.8 slice.21
  11.5 3.3 %collective-permute-start.1 = (bf16[64,512]{1,0:T(8,128)(2,1)S(1)}, bf16[64,512]{1,0:T(8,128)(2,1)S(1)}, u32[]{:S(2)}, u32[]{:S(2)}) collective-permute-start(bf16[64,512]{1,0:T(8,128)(2,1)S(1)} %slice.21), channel_id=1, source_target_pairs={{4,0},{8,4},{12,8},{16,12},{20,16},{24,20},{28,24},{5,1},{9,5},{13... | collective-permute-start | bytes 196616 | tf_op jit(solution)/shard_map/ppermute | solution.py:12
  14.8 0.1 slice.24
  14.9 2.3 slice.20
  17.1 0.0 collective-permute-done
  17.2 0.8 convert_reduce_fusion.2
  18.0 0.0 collective-permute-done.1
  18.0 5.2 %convert_reduce_fusion.1 = (f32[512]{0:T(512)S(1)}, bf16[3584,512]{1,0:T(8,128)(2,1)}, f32[512]{0:T(512)S(1)}) fusion(bf16[3584,512]{1,0:T(8,128)(2,1)S(1)} %copy-done, pred[3584]{0:T(1024)(128)(4,1)S(1)} %get-tuple-element.6, bf16[64,512]{1,0:T(8,128)(2,1)S(1)} %collective-permute-done.1, bf16[3520,512]{1,0:T(8,128)(2,1)S(1)} %slice.20), kind=kLoop, calls=%fused_computation.7 | loop fusion | flops 18349056 | bytes 11017728 | tf_op jit(solution)/shard_map/reduce_sum | solution.py:26
  23.2 0.0 all-gather.3.cloned.1.call-update
  23.2 0.0 reduce-scatter.2.cloned.1.call-start
  23.3 95.1 %all-gather.3.cloned.1.call-done = bf16[3584,2048]{1,0:T(8,128)(2,1)} async-done(((bf16[3584,512]{1,0:T(8,128)(2,1)}), bf16[3584,2048]{1,0:T(8,128)(2,1)}) %all-gather.3.cloned.1.call-update) | async-done | bytes 14680080 | tf_op jit(solution)/shard_map/all_gather | solution.py:30
  118.3 22.9 %fusion = f32[2048,1024]{1,0:T(8,128)} fusion(bf16[3584,2048]{1,0:T(8,128)(2,1)} %all-gather.3.cloned.1.call-done, bf16[64,512]{1,0:T(8,128)(2,1)S(1)} %collective-permute-done.1, bf16[3520,512]{1,0:T(8,128)(2,1)} %copy-done.1, bf16[3584,512]{1,0:T(8,128)(2,1)} %get-tuple-element.8), kind=kOutput, calls=%fused_computation | convolution fusion | flops 15054405632 | bytes 30408704 | tf_op jit(solution)/shard_map/dot_general | solution.py:29
  141.2 0.0 reduce-scatter.2.cloned.1.call-update
  141.2 18.3 %all-reduce = (f32[512]{0:T(512)S(1)}, f32[]{:T(128)}, f32[512]{0:T(512)S(1)}) all-reduce(f32[512]{0:T(512)S(1)} %get-tuple-element.7, f32[]{:T(128)} %get-tuple-element.5, f32[512]{0:T(512)S(1)} %get-tuple-element.11), channel_id=1, replica_groups=mesh['frames'=8,'blocks'=4] {'frames'}, use_global_device_ids=true, to_apply=%region_4.5 | all-reduce | flops 1025 | bytes 8200 | tf_op jit(solution)/shard_map/psum | solution.py:40
  159.5 0.6 broadcast_divide_fusion.1
  160.1 5.2 %all-gather = f32[4,1,512]{2,1,0:T(1,128)S(1)} all-gather(f32[1,1,512]{2,1,0:T(1,128)S(1)} %bitcast.3), channel_id=1, replica_groups=mesh['frames'=8,'blocks'=4] {'blocks'}, dimensions={0}, use_global_device_ids=true | all-gather | bytes 10240 | tf_op jit(solution)/shard_map/all_gather | solution.py:43
  165.2 0.1 dynamic_slice.3
  165.3 0.6 broadcast_divide_fusion
  165.9 122.0 %reduce-scatter.2.cloned.1.call-done = f32[256,1024]{1,0:T(8,128)} async-done(((f32[2048,1024]{1,0:T(8,128)}), f32[256,1024]{1,0:T(8,128)}) %reduce-scatter.2.cloned.1.call-update) | async-done | bytes 1048592 | tf_op jit(solution)/shard_map/reduce_scatter | solution.py:35
  287.9 2.9 fusion.6
  (6 shorter events, 0.0 us)
Async XLA Ops:
  7.2 10.0 %copy-start.2 = (s32[3584]{0:T(1024)S(1)}, s32[3584]{0:T(1024)}, u32[]{:S(2)}) copy-start(s32[3584]{0:T(1024)} %param.3) | copy-start | bytes 43012
  7.2 111.2 %all-gather.3.cloned.1.call-start = ((), (), s32[]{:S(2)}) async-start(), calls=%async_computation.1 | async-start | bytes 18350080 | tf_op jit(solution)/shard_map/all_gather | solution.py:30
  7.2 10.8 %copy-start = (bf16[3584,512]{1,0:T(8,128)(2,1)S(1)}, bf16[3584,512]{1,0:T(8,128)(2,1)}, u32[]{:S(2)}) copy-start(bf16[3584,512]{1,0:T(8,128)(2,1)} %param.2) | copy-start | bytes 11010052
  8.1 9.0 %collective-permute-start = (s32[64]{0:T(128)S(1)}, s32[64]{0:T(128)S(1)}, u32[]{:S(2)}, u32[]{:S(2)}) collective-permute-start(s32[64]{0:T(128)S(1)} %slice.25), channel_id=1, source_target_pairs={{4,0},{8,4},{12,8},{16,12},{20,16},{24,20},{28,24},{5,1},{9,5},{13... | collective-permute-start | bytes 776 | tf_op jit(solution)/shard_map/ppermute | solution.py:12
  11.5 6.5 %collective-permute-start.1 = (bf16[64,512]{1,0:T(8,128)(2,1)S(1)}, bf16[64,512]{1,0:T(8,128)(2,1)S(1)}, u32[]{:S(2)}, u32[]{:S(2)}) collective-permute-start(bf16[64,512]{1,0:T(8,128)(2,1)S(1)} %slice.21), channel_id=1, source_target_pairs={{4,0},{8,4},{12,8},{16,12},{20,16},{24,20},{28,24},{5,1},{9,5},{13... | collective-permute-start | bytes 196616 | tf_op jit(solution)/shard_map/ppermute | solution.py:12
  17.1 6.0 %copy-start.1 = (bf16[3520,512]{1,0:T(8,128)(2,1)}, bf16[3520,512]{1,0:T(8,128)(2,1)S(1)}, u32[]{:S(2)}) copy-start(bf16[3520,512]{1,0:T(8,128)(2,1)S(1)} %slice.20) | copy-start | bytes 10813444
  23.2 264.7 %reduce-scatter.2.cloned.1.call-start = ((), (), s32[]{:S(2)}) async-start(), calls=%async_computation.2 | async-start | bytes 9437184 | tf_op jit(solution)/shard_map/reduce_scatter | solution.py:35
Sparse Core Ops, SparseCore 0:
  23.3 94.9 all-gather.2
  141.4 146.4 reduce-scatter.1
where the time goes:
time: 302 us; the launch traced here: 298 us
  waiting for transfers between devices  217 us (72%)
  blocking collectives  23.4 us (8%)
  matrix products  22.9 us (8%)
  between operations  14.1 us (5%)
  other arithmetic  10.9 us (4%)
  starting transfers between devices  5.91 us (2%)
  local copies, waits for them, and re-layouts  3.27 us (1%)
    reduce_scatter x1, waiting for transfers between devices, shards(): reduced = lax.psum_scatter(terms, 'frames', scatter_dimension=0, tiled=True)  122 us
    all_gather x1, waiting for transfers between devices, shards(): lax.all_gather(current, 'blocks', axis=1, tiled=True)  95.1 us
    dot_general x1, matrix products, shards(): lax.dot_general(lax.all_gather(current, 'blocks', axis=1, tiled=True), bo...  22.9 us
    psum x1, blocking collectives, shards(): lax.psum((sums_zero, sums_lag, count_local), 'frames')  18.3 us
  transfers between devices with their start and end apart: 4, of which 2 were waited for; matrix products, arithmetic and copies ran while one was open for 2% of the time, Pallas kernels for 0%

commit v1 on v0

v1 whole, which is shorter than its diff:
```python
import functools

import jax
import jax.numpy as jnp
from jax import lax
from jax.experimental import pallas as pl
from jax.experimental.pallas import tpu as pltpu
from jax.sharding import PartitionSpec as P

LAG = 64
EXTRA = 8
BEHIND = 2
MESH = pl.DeviceIdType.MESH
OVER_FRAMES = (((0,), (0,)), ((), ()))


def flip(i):
    return i + 1 - 2 * lax.rem(i, 2)


def kernel(n, m, cw, x_ref, ids_ref, out_ref, xall, xo, wide, ids, marks, base, tb, rx, rz,
           load_sem, halo_send, halo_recv, gsend, psend, fsend, grecv, xsend, xrecv, zsend, zrecv):
    f = lax.axis_index("frames")
    b = lax.axis_index("blocks")
    total, own = x_ref.shape
    gw = 2 * cw
    rb = own // 2
    parts = rb // cw
    peers = m // 2 - 1
    steps = m * parts
    side = lax.rem(f, 2)
    group = lax.div(f, 2)
    mate = flip(b)
    before = lax.rem(f + n - 1, n)
    after = lax.rem(f + 1, n)

    def peer(i):
        return lax.rem(b + 2 * (i + 1), m)

    loads = []
    for j in range(parts):
        if parts == 1:
            loads.append([pltpu.make_async_copy(x_ref, xall.at[b, j], load_sem.at[2 * j])])
        else:
            loads.append([
                pltpu.make_async_copy(
                    x_ref.at[:, pl.ds(half * rb + j * cw, cw)],
                    xall.at[b, j, :, pl.ds(half * cw, cw)],
                    load_sem.at[2 * j + half],
                )
                for half in range(2)
            ])
    natural = pltpu.make_async_copy(x_ref, xo.at[pl.ds(0, total)], load_sem.at[2 * parts])
    numbers = pltpu.make_async_copy(ids_ref, ids.at[pl.ds(0, total)], load_sem.at[2 * parts + 1])
    for copies in loads:
        for copy in copies:
            copy.start()
    natural.start()
    numbers.start()

    barrier = pltpu.get_barrier_semaphore()

    def greet(to_frames, to_blocks):
        pl.semaphore_signal(barrier, inc=1, device_id=(to_frames, to_blocks), device_id_type=MESH)

    greet(before, b)
    greet(after, b)
    greet(flip(f), b)
    greet(f, mate)
    for i in range(peers):
        greet(f, peer(i))
    for i in range(1, m):
        greet(2 * lax.rem(group + i, m) + side, b)
    pl.semaphore_wait(barrier, 4 + peers + m - 1)

    halo = [
        pltpu.make_async_remote_copy(
            x_ref.at[pl.ds(0, LAG)], xo.at[pl.ds(total, LAG)], halo_send.at[0], halo_recv.at[0],
            device_id=(before, b), device_id_type=MESH),
        pltpu.make_async_remote_copy(
            ids_ref.at[pl.ds(0, LAG)], ids.at[pl.ds(total, LAG)], halo_send.at[1], halo_recv.at[1],
            device_id=(before, b), device_id_type=MESH),
    ]
    for copy in halo:
        copy.start()

    def to_peer(i, j):
        return pltpu.make_async_remote_copy(
            xall.at[b, j], xall.at[b, j], gsend.at[i, j], grecv.at[b, j],
            device_id=(f, peer(i)), device_id_type=MESH)

    def to_mate(j):
        return pltpu.make_async_remote_copy(
            xall.at[b, j], xall.at[b, j], psend.at[j], grecv.at[b, j],
            device_id=(f, mate), device_id_type=MESH)

    def onward(i, j):
        source = peer(i)
        return pltpu.make_async_remote_copy(
            xall.at[source, j], xall.at[source, j], fsend.at[i, j], grecv.at[source, j],
            device_id=(f, mate), device_id_type=MESH)

    def arrival(source, j):
        return pltpu.make_async_remote_copy(
            xall.at[source, j], xall.at[source, j], psend.at[j], grecv.at[source, j],
            device_id=(f, mate), device_id_type=MESH)

    for j in range(parts):
        for copy in loads[j]:
            copy.wait()
        for i in range(peers):
            to_peer(i, j).start()
        to_mate(j).start()

    natural.wait()
    numbers.wait()
    for copy in halo:
        copy.wait()

    tile = LAG
    last = jnp.where(f == n - 1, total - LAG, total)

    def mask_rows(t, count):
        at = pl.multiple_of(t * tile, tile)
        here = ids[pl.ds(at, tile), :]
        there = ids[pl.ds(at + LAG, tile), :]
        row = at + lax.broadcasted_iota(jnp.int32, here.shape, 0)
        mark = jnp.where((here == there) & (row < last), 1.0, 0.0)
        mark16 = mark.astype(jnp.bfloat16)
        marks[pl.ds(at, tile), :] = mark16
        for c in range(own // 128):
            lanes = slice(c * 128, (c + 1) * 128)
            wide[pl.ds(at, tile), lanes] = xo[pl.ds(at, tile), lanes] * mark16
            wide[pl.ds(at, tile), own + c * 128:own + (c + 1) * 128] = (
                xo[pl.ds(at + LAG, tile), lanes] * mark16)
        return count + jnp.sum(mark, axis=0, keepdims=True)

    count = lax.fori_loop(0, total // tile, mask_rows, jnp.zeros((1, 128), jnp.float32))
    column_sums = lax.dot_general(
        marks[...], wide[...], OVER_FRAMES, preferred_element_type=jnp.float32)[0:EXTRA]
    row_of = lax.broadcasted_iota(jnp.int32, (EXTRA, 2 * own), 0)
    base[...] = jnp.where(row_of == 0, column_sums, 0.0)
    for c in range(2 * own // 128):
        lanes = slice(c * 128, (c + 1) * 128)
        base[:, lanes] = jnp.where(row_of[:, lanes] == 2, count, base[:, lanes])

    def place(k):
        j = lax.rem(k, parts)
        near = k < 2 * parts
        later_k = jnp.maximum(k - 2 * parts, 0)
        turn = lax.div(later_k, 2)
        i = lax.div(turn, parts)
        far = lax.rem(b + 2 * (i + 1), m)
        forwarded = lax.rem(later_k, 2)
        far_block = jnp.where(forwarded == 1, flip(far), far)
        near_block = jnp.where(k < parts, b, mate)
        return (jnp.where(near, near_block, far_block),
                jnp.where(near, j, lax.rem(turn, parts)), i, forwarded)

    def pair_copy(block, j):
        return pltpu.make_async_remote_copy(
            tb.at[block, j, 1 - side], rx.at[block, j], xsend.at[block, j], xrecv.at[block, j],
            device_id=(flip(f), b), device_id_type=MESH)

    def group_copy(block, j):
        return pltpu.make_async_remote_copy(
            tb.at[block, j, side], rz.at[group, j], zsend.at[block, j], zrecv.at[group, j],
            device_id=(2 * block + side, b), device_id_type=MESH)

    def step(k, carry):
        @pl.when(k < steps)
        def _():
            block, j, i, forwarded = place(k)

            @pl.when(k >= parts)
            def _():
                arrival(block, j).wait_recv()

            @pl.when((k >= 2 * parts) & (forwarded == 0))
            def _():
                onward(i, j).start()

            depth = total // 4
            for q in range(4):
                rows = slice(q * depth, (q + 1) * depth)
                granule = xall[block, j, rows, :]
                terms = lax.dot_general(
                    granule, wide[rows, :], OVER_FRAMES, preferred_element_type=jnp.float32)
                sums = lax.dot_general(
                    marks[rows, :], granule, OVER_FRAMES,
                    preferred_element_type=jnp.float32)[0:EXTRA]
                sums = jnp.where(lax.broadcasted_iota(jnp.int32, sums.shape, 0) == 1, sums, 0.0)
                for half in range(2):
                    value = terms[half * cw:(half + 1) * cw]
                    if q == 0:
                        tb[block, j, half, 0:cw, :] = value
                        tb[block, j, half, cw:cw + EXTRA, :] = base[...]
                    else:
                        tb[block, j, half, 0:cw, :] += value
                    tb[block, j, half, cw:cw + EXTRA, 0:gw] += sums
            pair_copy(block, j).start()

        @pl.when(k >= BEHIND)
        def _():
            block, j, _i, _forwarded = place(k - BEHIND)
            pair_copy(block, j).wait_recv()
            tb[block, j, side] += rx[block, j]

            @pl.when(block != group)
            def _():
                group_copy(block, j).start()

        return carry

    lax.fori_loop(0, steps + BEHIND, step, 0)

    for j in range(parts):
        out_ref[j] = tb[group, j, side]
        for i in range(1, m):
            source = lax.rem(group + i, m)
            pltpu.make_async_remote_copy(
                rz.at[source, j], rz.at[source, j], zsend.at[source, j], zrecv.at[source, j],
                device_id=(2 * source + side, b), device_id_type=MESH).wait_recv()
            out_ref[j] += rz[source, j]

    for j in range(parts):
        to_mate(j).wait_send()
        for i in range(peers):
            to_peer(i, j).wait_send()
            onward(i, j).wait_send()
        for i in range(m):
            pair_copy(i, j).wait_send()
        for i in range(1, m):
            group_copy(lax.rem(group + i, m), j).wait_send()


def shards(n, m, frames_data, traj_ids):
    total, own = frames_data.shape
    rb = own * m // n
    assert n == 2 * m and own == 2 * rb
    cw = min(128, rb)
    parts = rb // cw
    ids = jnp.broadcast_to(traj_ids[:, None], (total, 128))
    piece = (cw + EXTRA, 2 * own)
    sem = pltpu.SemaphoreType.DMA
    peers = m // 2 - 1
    reduced = pl.pallas_call(
        functools.partial(kernel, n, m, cw),
        out_shape=jax.ShapeDtypeStruct((parts, *piece), jnp.float32),
        in_specs=[pl.BlockSpec(memory_space=pl.ANY)] * 2,
        out_specs=pl.BlockSpec(memory_space=pltpu.VMEM),
        scratch_shapes=[
            pltpu.VMEM((m, parts, total, 2 * cw), jnp.bfloat16),
            pltpu.VMEM((total + LAG, own), jnp.bfloat16),
            pltpu.VMEM((total, 2 * own), jnp.bfloat16),
            pltpu.VMEM((total + LAG, 128), jnp.int32),
            pltpu.VMEM((total, 128), jnp.bfloat16),
            pltpu.VMEM((EXTRA, 2 * own), jnp.float32),
            pltpu.VMEM((m, parts, 2, *piece), jnp.float32),
            pltpu.VMEM((m, parts, *piece), jnp.float32),
            pltpu.VMEM((m, parts, *piece), jnp.float32),
            sem((2 * parts + 2,)),
            sem((2,)),
            sem((2,)),
            sem((peers, parts)),
            sem((parts,)),
            sem((peers, parts)),
            sem((m, parts)),
            sem((m, parts)),
            sem((m, parts)),
            sem((m, parts)),
            sem((m, parts)),
        ],
        compiler_params=pltpu.CompilerParams(
            collective_id=0, has_side_effects=True, vmem_limit_bytes=58 * 2**20),
        cost_estimate=pl.CostEstimate(
            flops=4 * total * own * own * m, bytes_accessed=4 * total * own, transcendentals=0),
    )(frames_data, ids)
    side = lax.axis_index("frames") % 2
    count = reduced[0, cw + 2, 0]
    terms = reduced[:, :cw].reshape(rb, 2 * own)
    column_means = reduced[0, cw] / count
    row_sums = lax.dynamic_slice_in_dim(reduced[:, cw + 1], side * cw, cw, 1).reshape(rb)
    cov = terms / count - (row_sums / count)[:, None] * column_means[None, :]
    return cov[:, :own], cov[:, own:]


def solution(mesh):
    n, m = mesh.shape["frames"], mesh.shape["blocks"]
    return jax.shard_map(
        functools.partial(shards, n, m),
        mesh=mesh,
        in_specs=(P("frames", "blocks"), P("frames")),
        out_specs=(P("frames", "blocks"), P("frames", "blocks")),
        check_vma=False,
    )
```

time: 302 us -> 195 us (0.65); the launches traced: 298 us -> 194 us
  waiting for transfers between devices: 217 us -> 0 us
  Pallas kernels: 0 us -> 183 us
  blocking collectives: 23.4 us -> 0 us
  matrix products: 22.9 us -> 0 us
  between operations: 14.1 us -> 0.66 us
  other arithmetic: 10.9 us -> 4.22 us
  starting transfers between devices: 5.91 us -> 0 us
    pallas_call x0 -> x1, Pallas kernels: none -> 183 us  [shards(): pl.pallas_call(functools.partial(kernel, n, m, cw), out_shape=jax.ShapeDt...]
    reduce_scatter x1 -> x0, waiting for transfers between devices: 122 us -> none  [shards(): reduced = lax.psum_scatter(terms, 'frames', scatter_dimension=0, tiled=True)]
    all_gather x1 -> x0, waiting for transfers between devices: 95.1 us -> none  [shards(): lax.all_gather(current, 'blocks', axis=1, tiled=True)]
    dot_general x1 -> x0, matrix products: 22.9 us -> none  [shards(): lax.dot_general(lax.all_gather(current, 'blocks', axis=1, tiled=True), bo...]
    psum x1 -> x0, blocking collectives: 18.3 us -> none  [shards(): lax.psum((sums_zero, sums_lag, count_local), 'frames')]
    reduce_sum x2 -> x0, other arithmetic: 6.01 us -> none  [the longest x1 5.16 us: shards(): sums_zero = jnp.sum(current.astype(jnp.float32), axis=0)]
    ppermute x2 -> x0, starting transfers between devices: 5.83 us -> none  [shifted(): lax.ppermute(value, axis, [(source, source + steps) for source in range(f...]
    all_gather x1 -> x0, blocking collectives: 5.16 us -> none  [shards(): mean_all = lax.all_gather(mean_cols, 'blocks', axis=0, tiled=True)]
  transfers between devices with their start and end apart: 4 -> 0, of which waited for: 2 -> 0; matrix products, arithmetic and copies ran while one was open for 2% -> 0% of each run, Pallas kernels for 0% -> 0%
where the time goes in v1:
time: 195 us; the launch traced here: 194 us
  Pallas kernels  183 us (94%)
  local copies, waits for them, and re-layouts  6.09 us (3%)
  other arithmetic  4.22 us (2%)
    pallas_call x1, Pallas kernels, shards(): pl.pallas_call(functools.partial(kernel, n, m, cw), out_shape=jax.ShapeDt...  183 us

profile of v1, /device:TPU:26, one launch (start us, length us, event | category | flops | bytes accessed | tf_op | source)
XLA Modules:
  0.0 194.3 jit_solution(12838028434014486751)
XLA Ops:
  0.6 3.0 %broadcast_in_dim.2.ids_ref = s32[3584,128]{1,0:T(8,128)} broadcast(s32[3584]{0:T(1024)} %param.3), dimensions={0} | broadcast | bytes 1849344 | tf_op jit(solution)/shard_map/broadcast_in_dim | solution.py:243
  3.6 183.3 %shard_map.41 = f32[2,136,1024]{2,1,0:T(8,128)} custom-call(bf16[3584,512]{1,0:T(8,128)(2,1)} %x_ref.1, s32[3584,128]{1,0:T(8,128)} %broadcast_in_dim.2.ids_ref), custom_call_target="tpu_custom_call" | custom-call | flops 15032385536 | bytes 7340032 | tf_op jit(solution)/shard_map/pallas_call | solution.py:247
  186.9 1.2 slice.19
  188.1 2.0 %slice_divide_fusion = f32[2,128,1024]{2,1,0:T(8,128)S(1)} fusion(f32[2,136,1024]{2,1,0:T(8,128)} %shard_map.41, f32[]{:T(128)} %bitcast), kind=kLoop, calls=%fused_computation.1 | loop fusion | flops 262144 | bytes 2097156 | tf_op jit(solution)/shard_map/div | solution.py:284
  190.1 1.4 slice_divide_fusion.1
  191.5 0.9 slice.20
  192.4 0.7 dynamic-slice_divide_fusion
  193.0 0.2 bitcast_subtract_fusion
  193.2 1.0 fusion

commit v2 on v1

--- a/solution.py
+++ b/solution.py
@@ -9,7 +9,6 @@
 
 LAG = 64
 EXTRA = 8
-BEHIND = 2
 MESH = pl.DeviceIdType.MESH
 OVER_FRAMES = (((0,), (0,)), ((), ()))
 
@@ -19,7 +18,7 @@
 
 
 def kernel(n, m, cw, x_ref, ids_ref, out_ref, xall, xo, wide, ids, marks, base, tb, rx, rz,
-           load_sem, halo_send, halo_recv, gsend, psend, fsend, grecv, xsend, xrecv, zsend, zrecv):
+           load_sem, halo_send, halo_recv, hsend, psend, fsend, mrecv, hrecv, xsend, xrecv, zsend, zrecv):
     f = lax.axis_index("frames")
     b = lax.axis_index("blocks")
     total, own = x_ref.shape
@@ -30,12 +29,22 @@
     steps = m * parts
     side = lax.rem(f, 2)
     group = lax.div(f, 2)
+    levels = m.bit_length() - 1
+    core = lax.rem(b, 2)
+    chip = lax.div(b, 2)
+    span = total // 2
     mate = flip(b)
     before = lax.rem(f + n - 1, n)
     after = lax.rem(f + 1, n)
 
     def peer(i):
         return lax.rem(b + 2 * (i + 1), m)
+
+    def bit(i, p):
+        return lax.rem(lax.div(i, 2**p), 2)
+
+    def across(p):
+        return group + 2**p - 2 ** (p + 1) * bit(group, p)
 
     loads = []
     for j in range(parts):
@@ -69,9 +78,9 @@
     greet(f, mate)
     for i in range(peers):
         greet(f, peer(i))
-    for i in range(1, m):
-        greet(2 * lax.rem(group + i, m) + side, b)
-    pl.semaphore_wait(barrier, 4 + peers + m - 1)
+    for p in range(levels):
+        greet(2 * across(p) + side, b)
+    pl.semaphore_wait(barrier, 4 + peers + levels)
 
     halo = [
         pltpu.make_async_remote_copy(
@@ -84,34 +93,50 @@
     for copy in halo:
         copy.start()
 
-    def to_peer(i, j):
-        return pltpu.make_async_remote_copy(
-            xall.at[b, j], xall.at[b, j], gsend.at[i, j], grecv.at[b, j],
+    def part(block, j, which):
+        return xall.at[block, j, pl.ds(pl.multiple_of(which * span, 16), span)]
+
+    def to_peer(i, j, e):
+        block = 2 * chip + e
+        return pltpu.make_async_remote_copy(
+            part(block, j, core), part(block, j, core), hsend.at[i, j, e], hrecv.at[block, j, core],
             device_id=(f, peer(i)), device_id_type=MESH)
 
     def to_mate(j):
         return pltpu.make_async_remote_copy(
-            xall.at[b, j], xall.at[b, j], psend.at[j], grecv.at[b, j],
+            xall.at[b, j], xall.at[b, j], psend.at[j], mrecv.at[j],
             device_id=(f, mate), device_id_type=MESH)
 
-    def onward(i, j):
-        source = peer(i)
-        return pltpu.make_async_remote_copy(
-            xall.at[source, j], xall.at[source, j], fsend.at[i, j], grecv.at[source, j],
+    def from_mate(j):
+        return pltpu.make_async_remote_copy(
+            xall.at[mate, j], xall.at[mate, j], psend.at[j], mrecv.at[j],
             device_id=(f, mate), device_id_type=MESH)
 
-    def arrival(source, j):
-        return pltpu.make_async_remote_copy(
-            xall.at[source, j], xall.at[source, j], psend.at[j], grecv.at[source, j],
+    def onward(block, j):
+        return pltpu.make_async_remote_copy(
+            part(block, j, core), part(block, j, core), fsend.at[block, j], hrecv.at[block, j, core],
             device_id=(f, mate), device_id_type=MESH)
+
+    def arrival(block, j, which):
+        return pltpu.make_async_remote_copy(
+            part(block, j, which), part(block, j, which), fsend.at[block, j],
+            hrecv.at[block, j, which], device_id=(f, mate), device_id_type=MESH)
 
     for j in range(parts):
         for copy in loads[j]:
             copy.wait()
-        for i in range(peers):
-            to_peer(i, j).start()
         to_mate(j).start()
 
+    def spread(j):
+        for e in range(2):
+            @pl.when(core != e)
+            def _():
+                from_mate(j).wait_recv()
+
+            for i in range(peers):
+                to_peer(i, j, e).start()
+
+    spread(0)
     natural.wait()
     numbers.wait()
     for copy in halo:
@@ -144,41 +169,65 @@
         lanes = slice(c * 128, (c + 1) * 128)
         base[:, lanes] = jnp.where(row_of[:, lanes] == 2, count, base[:, lanes])
 
+    for j in range(1, parts):
+        spread(j)
+
     def place(k):
         j = lax.rem(k, parts)
         near = k < 2 * parts
         later_k = jnp.maximum(k - 2 * parts, 0)
         turn = lax.div(later_k, 2)
-        i = lax.div(turn, parts)
-        far = lax.rem(b + 2 * (i + 1), m)
-        forwarded = lax.rem(later_k, 2)
-        far_block = jnp.where(forwarded == 1, flip(far), far)
+        far = lax.rem(chip + lax.div(turn, parts) + 1, m // 2)
+        far_block = 2 * far + lax.rem(later_k, 2)
         near_block = jnp.where(k < parts, b, mate)
-        return (jnp.where(near, near_block, far_block),
-                jnp.where(near, j, lax.rem(turn, parts)), i, forwarded)
+        return jnp.where(near, near_block, far_block), jnp.where(near, j, lax.rem(turn, parts))
 
     def pair_copy(block, j):
         return pltpu.make_async_remote_copy(
             tb.at[block, j, 1 - side], rx.at[block, j], xsend.at[block, j], xrecv.at[block, j],
             device_id=(flip(f), b), device_id_type=MESH)
 
-    def group_copy(block, j):
-        return pltpu.make_async_remote_copy(
-            tb.at[block, j, side], rz.at[group, j], zsend.at[block, j], zrecv.at[group, j],
-            device_id=(2 * block + side, b), device_id_type=MESH)
+    def group_copy(block, j, p):
+        return pltpu.make_async_remote_copy(
+            tb.at[block, j, side], rz.at[block, j, p], zsend.at[block, j], zrecv.at[block, j, p],
+            device_id=(2 * across(p) + side, b), device_id_type=MESH)
+
+    def stage(p, q, carry):
+        block, j = place(q)
+
+        @pl.when(lax.rem(group, 2**p) == lax.rem(block, 2**p))
+        def _():
+            if p == 0:
+                pair_copy(block, j).wait_recv()
+                tb[block, j, side] += rx[block, j]
+            else:
+                group_copy(block, j, p - 1).wait_recv()
+                tb[block, j, side] += rz[block, j, p - 1]
+            if p < levels:
+                @pl.when(bit(group, p) != bit(block, p))
+                def _():
+                    group_copy(block, j, p).start()
+
+        return carry
+
+    def finished(p, k):
+        usual = jnp.maximum(k - 1 - p, 0)
+        eager = jnp.where(k == steps - 1, jnp.maximum(steps - 1 - p, 0), usual)
+        return jnp.where(k < 0, 0, jnp.where(k >= steps, steps, eager))
 
     def step(k, carry):
+        for p in range(levels + 1):
+            lax.fori_loop(finished(p, k - 1), finished(p, k), functools.partial(stage, p), 0)
+
         @pl.when(k < steps)
         def _():
-            block, j, i, forwarded = place(k)
-
-            @pl.when(k >= parts)
+            block, j = place(k)
+
+            @pl.when(k >= 2 * parts)
             def _():
-                arrival(block, j).wait_recv()
-
-            @pl.when((k >= 2 * parts) & (forwarded == 0))
-            def _():
-                onward(i, j).start()
+                arrival(block, j, core).wait_recv()
+                onward(block, j).start()
+                arrival(block, j, 1 - core).wait_recv()
 
             depth = total // 4
             for q in range(4):
@@ -200,44 +249,31 @@
                     tb[block, j, half, cw:cw + EXTRA, 0:gw] += sums
             pair_copy(block, j).start()
 
-        @pl.when(k >= BEHIND)
-        def _():
-            block, j, _i, _forwarded = place(k - BEHIND)
-            pair_copy(block, j).wait_recv()
-            tb[block, j, side] += rx[block, j]
-
-            @pl.when(block != group)
-            def _():
-                group_copy(block, j).start()
-
         return carry
 
-    lax.fori_loop(0, steps + BEHIND, step, 0)
-
+    lax.fori_loop(0, steps, step, 0)
+    for p in range(levels + 1):
+        lax.fori_loop(finished(p, steps - 1), steps, functools.partial(stage, p), 0)
     for j in range(parts):
         out_ref[j] = tb[group, j, side]
-        for i in range(1, m):
-            source = lax.rem(group + i, m)
-            pltpu.make_async_remote_copy(
-                rz.at[source, j], rz.at[source, j], zsend.at[source, j], zrecv.at[source, j],
-                device_id=(2 * source + side, b), device_id_type=MESH).wait_recv()
-            out_ref[j] += rz[source, j]
 
     for j in range(parts):
         to_mate(j).wait_send()
         for i in range(peers):
-            to_peer(i, j).wait_send()
-            onward(i, j).wait_send()
+            for e in range(2):
+                to_peer(i, j, e).wait_send()
+                onward(2 * lax.rem(chip + i + 1, m // 2) + e, j).wait_send()
         for i in range(m):
             pair_copy(i, j).wait_send()
         for i in range(1, m):
-            group_copy(lax.rem(group + i, m), j).wait_send()
+            group_copy(lax.rem(group + i, m), j, 0).wait_send()
 
 
 def shards(n, m, frames_data, traj_ids):
     total, own = frames_data.shape
     rb = own * m // n
-    assert n == 2 * m and own == 2 * rb
+    levels = m.bit_length() - 1
+    assert n == 2 * m and own == 2 * rb and m == 2**levels
     cw = min(128, rb)
     parts = rb // cw
     ids = jnp.broadcast_to(traj_ids[:, None], (total, 128))
@@ -258,18 +294,19 @@
             pltpu.VMEM((EXTRA, 2 * own), jnp.float32),
             pltpu.VMEM((m, parts, 2, *piece), jnp.float32),
             pltpu.VMEM((m, parts, *piece), jnp.float32),
-            pltpu.VMEM((m, parts, *piece), jnp.float32),
+            pltpu.VMEM((m, parts, levels, *piece), jnp.float32),
             sem((2 * parts + 2,)),
             sem((2,)),
             sem((2,)),
-            sem((peers, parts)),
+            sem((peers, parts, 2)),
             sem((parts,)),
-            sem((peers, parts)),
+            sem((m, parts)),
+            sem((parts,)),
+            sem((m, parts, 2)),
             sem((m, parts)),
             sem((m, parts)),
             sem((m, parts)),
-            sem((m, parts)),
-            sem((m, parts)),
+            sem((m, parts, levels)),
         ],
         compiler_params=pltpu.CompilerParams(
             collective_id=0, has_side_effects=True, vmem_limit_bytes=58 * 2**20),

time: 195 us -> 169 us (0.87)
  Pallas kernels: 183 us -> 156 us
    pallas_call x1, Pallas kernels: 183 us -> 156 us  [shards(): pl.pallas_call(functools.partial(kernel, n, m, cw), out_shape=jax.ShapeDt...]
where the time goes in v2:
time: 169 us; the launch traced here: 167 us
  Pallas kernels  156 us (92%)
  local copies, waits for them, and re-layouts  6.09 us (4%)
  other arithmetic  4.22 us (2%)
    pallas_call x1, Pallas kernels, shards(): pl.pallas_call(functools.partial(kernel, n, m, cw), out_shape=jax.ShapeDt...  156 us

profile of v2, /device:TPU:26, one launch (start us, length us, event | category | flops | bytes accessed | tf_op | source)
XLA Modules:
  0.0 166.6 jit_solution(9310469559578151753)
XLA Ops:
  0.6 3.0 %broadcast_in_dim.2.ids_ref = s32[3584,128]{1,0:T(8,128)} broadcast(s32[3584]{0:T(1024)} %param.3), dimensions={0} | broadcast | bytes 1849344 | tf_op jit(solution)/shard_map/broadcast_in_dim | solution.py:279
  3.6 155.6 %shard_map.41 = f32[2,136,1024]{2,1,0:T(8,128)} custom-call(bf16[3584,512]{1,0:T(8,128)(2,1)} %x_ref.1, s32[3584,128]{1,0:T(8,128)} %broadcast_in_dim.2.ids_ref), custom_call_target="tpu_custom_call" | custom-call | flops 15032385536 | bytes 7340032 | tf_op jit(solution)/shard_map/pallas_call | solution.py:283
  159.2 1.2 slice.19
  160.4 2.0 %slice_divide_fusion = f32[2,128,1024]{2,1,0:T(8,128)S(1)} fusion(f32[2,136,1024]{2,1,0:T(8,128)} %shard_map.41, f32[]{:T(128)} %bitcast), kind=kLoop, calls=%fused_computation.1 | loop fusion | flops 262144 | bytes 2097156 | tf_op jit(solution)/shard_map/div | solution.py:321
  162.4 1.4 slice_divide_fusion.1
  163.9 0.9 slice.20
  164.7 0.7 dynamic-slice_divide_fusion
  165.4 0.2 bitcast_subtract_fusion
  165.5 1.0 fusion

commit v3 on v2

--- a/solution.py
+++ b/solution.py
@@ -155,24 +155,26 @@
         marks[pl.ds(at, tile), :] = mark16
         for c in range(own // 128):
             lanes = slice(c * 128, (c + 1) * 128)
-            wide[pl.ds(at, tile), lanes] = xo[pl.ds(at, tile), lanes] * mark16
-            wide[pl.ds(at, tile), own + c * 128:own + (c + 1) * 128] = (
+            wide[0, pl.ds(at, tile), lanes] = xo[pl.ds(at, tile), lanes] * mark16
+            wide[1, pl.ds(at, tile), lanes] = (
                 xo[pl.ds(at + LAG, tile), lanes] * mark16)
         return count + jnp.sum(mark, axis=0, keepdims=True)
 
     count = lax.fori_loop(0, total // tile, mask_rows, jnp.zeros((1, 128), jnp.float32))
-    column_sums = lax.dot_general(
-        marks[...], wide[...], OVER_FRAMES, preferred_element_type=jnp.float32)[0:EXTRA]
-    row_of = lax.broadcasted_iota(jnp.int32, (EXTRA, 2 * own), 0)
-    base[...] = jnp.where(row_of == 0, column_sums, 0.0)
-    for c in range(2 * own // 128):
-        lanes = slice(c * 128, (c + 1) * 128)
-        base[:, lanes] = jnp.where(row_of[:, lanes] == 2, count, base[:, lanes])
+    row_of = lax.broadcasted_iota(jnp.int32, (EXTRA, own), 0)
+    for h in range(2):
+        column_sums = lax.dot_general(
+            marks[...], wide[h], OVER_FRAMES, preferred_element_type=jnp.float32)[0:EXTRA]
+        base[h] = jnp.where(row_of == 0, column_sums, 0.0)
+        for c in range(own // 128):
+            lanes = slice(c * 128, (c + 1) * 128)
+            base[h, :, lanes] = jnp.where(row_of[:, lanes] == 2, count, base[h, :, lanes])
 
     for j in range(1, parts):
         spread(j)
 
-    def place(k):
+    def place(u):
+        k = lax.div(u, 2)
         j = lax.rem(k, parts)
         near = k < 2 * parts
         later_k = jnp.maximum(k - 2 * parts, 0)
@@ -180,82 +182,86 @@
         far = lax.rem(chip + lax.div(turn, parts) + 1, m // 2)
         far_block = 2 * far + lax.rem(later_k, 2)
         near_block = jnp.where(k < parts, b, mate)
-        return jnp.where(near, near_block, far_block), jnp.where(near, j, lax.rem(turn, parts))
-
-    def pair_copy(block, j):
-        return pltpu.make_async_remote_copy(
-            tb.at[block, j, 1 - side], rx.at[block, j], xsend.at[block, j], xrecv.at[block, j],
+        return (jnp.where(near, near_block, far_block),
+                jnp.where(near, j, lax.rem(turn, parts)), lax.rem(u, 2))
+
+    def pair_copy(block, j, h):
+        return pltpu.make_async_remote_copy(
+            tb.at[block, j, h, 1 - side], rx.at[block, j, h], xsend.at[block, j, h], xrecv.at[block, j, h],
             device_id=(flip(f), b), device_id_type=MESH)
 
-    def group_copy(block, j, p):
-        return pltpu.make_async_remote_copy(
-            tb.at[block, j, side], rz.at[block, j, p], zsend.at[block, j], zrecv.at[block, j, p],
+    def group_copy(block, j, h, p):
+        return pltpu.make_async_remote_copy(
+            tb.at[block, j, h, side], rz.at[block, j, h, p], zsend.at[block, j, h], zrecv.at[block, j, h, p],
             device_id=(2 * across(p) + side, b), device_id_type=MESH)
 
     def stage(p, q, carry):
-        block, j = place(q)
+        block, j, h = place(q)
 
         @pl.when(lax.rem(group, 2**p) == lax.rem(block, 2**p))
         def _():
             if p == 0:
-                pair_copy(block, j).wait_recv()
-                tb[block, j, side] += rx[block, j]
+                pair_copy(block, j, h).wait_recv()
+                tb[block, j, h, side] += rx[block, j, h]
             else:
-                group_copy(block, j, p - 1).wait_recv()
-                tb[block, j, side] += rz[block, j, p - 1]
+                group_copy(block, j, h, p - 1).wait_recv()
+                tb[block, j, h, side] += rz[block, j, h, p - 1]
             if p < levels:
                 @pl.when(bit(group, p) != bit(block, p))
                 def _():
-                    group_copy(block, j, p).start()
+                    group_copy(block, j, h, p).start()
 
         return carry
 
     def finished(p, k):
-        usual = jnp.maximum(k - 1 - p, 0)
-        eager = jnp.where(k == steps - 1, jnp.maximum(steps - 1 - p, 0), usual)
-        return jnp.where(k < 0, 0, jnp.where(k >= steps, steps, eager))
+        return jnp.maximum(k - 1 - p, 0)
 
     def step(k, carry):
         for p in range(levels + 1):
             lax.fori_loop(finished(p, k - 1), finished(p, k), functools.partial(stage, p), 0)
 
-        @pl.when(k < steps)
+        block, j, h = place(k)
+
+        @pl.when((k >= 4 * parts) & (h == 0))
         def _():
-            block, j = place(k)
-
-            @pl.when(k >= 2 * parts)
-            def _():
-                arrival(block, j, core).wait_recv()
-                onward(block, j).start()
-                arrival(block, j, 1 - core).wait_recv()
-
-            depth = total // 4
-            for q in range(4):
-                rows = slice(q * depth, (q + 1) * depth)
-                granule = xall[block, j, rows, :]
-                terms = lax.dot_general(
-                    granule, wide[rows, :], OVER_FRAMES, preferred_element_type=jnp.float32)
-                sums = lax.dot_general(
-                    marks[rows, :], granule, OVER_FRAMES,
-                    preferred_element_type=jnp.float32)[0:EXTRA]
-                sums = jnp.where(lax.broadcasted_iota(jnp.int32, sums.shape, 0) == 1, sums, 0.0)
-                for half in range(2):
-                    value = terms[half * cw:(half + 1) * cw]
-                    if q == 0:
-                        tb[block, j, half, 0:cw, :] = value
-                        tb[block, j, half, cw:cw + EXTRA, :] = base[...]
-                    else:
-                        tb[block, j, half, 0:cw, :] += value
-                    tb[block, j, half, cw:cw + EXTRA, 0:gw] += sums
-            pair_copy(block, j).start()
-
+            arrival(block, j, core).wait_recv()
+            onward(block, j).start()
+            arrival(block, j, 1 - core).wait_recv()
+
+        depth = total // 4
+        for q in range(4):
+            rows = slice(q * depth, (q + 1) * depth)
+            granule = xall[block, j, rows, :]
+            terms = lax.dot_general(
+                granule, wide[h, rows, :], OVER_FRAMES, preferred_element_type=jnp.float32)
+            sums = lax.dot_general(
+                marks[rows, :], granule, OVER_FRAMES,
+                preferred_element_type=jnp.float32)[0:EXTRA]
+            sums = jnp.where(lax.broadcasted_iota(jnp.int32, sums.shape, 0) == 1, sums, 0.0)
+            for half in range(2):
+                value = terms[half * cw:(half + 1) * cw]
+                if q == 0:
+                    tb[block, j, h, half, 0:cw, :] = value
+                    tb[block, j, h, half, cw:cw + EXTRA, :] = base[h]
+                else:
+                    tb[block, j, h, half, 0:cw, :] += value
+                tb[block, j, h, half, cw:cw + EXTRA, 0:gw] += sums
+        pair_copy(block, j, h).start()
         return carry
 
-    lax.fori_loop(0, steps, step, 0)
-    for p in range(levels + 1):
-        lax.fori_loop(finished(p, steps - 1), steps, functools.partial(stage, p), 0)
+    units = 2 * steps
+    lax.fori_loop(0, units, step, 0)
+
+    def drain(k, carry):
+        for p in range(levels + 1):
+            lax.fori_loop(jnp.minimum(finished(p, k - 1), units), jnp.minimum(finished(p, k), units),
+                          functools.partial(stage, p), 0)
+        return carry
+
+    lax.fori_loop(units, units + levels + 2, drain, 0)
     for j in range(parts):
-        out_ref[j] = tb[group, j, side]
+        for h in range(2):
+            out_ref[j, :, h * own:(h + 1) * own] = tb[group, j, h, side]
 
     for j in range(parts):
         to_mate(j).wait_send()
@@ -263,10 +269,11 @@
             for e in range(2):
                 to_peer(i, j, e).wait_send()
                 onward(2 * lax.rem(chip + i + 1, m // 2) + e, j).wait_send()
-        for i in range(m):
-            pair_copy(i, j).wait_send()
-        for i in range(1, m):
-            group_copy(lax.rem(group + i, m), j, 0).wait_send()
+        for h in range(2):
+            for i in range(m):
+                pair_copy(i, j, h).wait_send()
+            for i in range(1, m):
+                group_copy(lax.rem(group + i, m), j, h, 0).wait_send()
 
 
 def shards(n, m, frames_data, traj_ids):
@@ -277,24 +284,24 @@
     cw = min(128, rb)
     parts = rb // cw
     ids = jnp.broadcast_to(traj_ids[:, None], (total, 128))
-    piece = (cw + EXTRA, 2 * own)
+    piece = (cw + EXTRA, own)
     sem = pltpu.SemaphoreType.DMA
     peers = m // 2 - 1
     reduced = pl.pallas_call(
         functools.partial(kernel, n, m, cw),
-        out_shape=jax.ShapeDtypeStruct((parts, *piece), jnp.float32),
+        out_shape=jax.ShapeDtypeStruct((parts, cw + EXTRA, 2 * own), jnp.float32),
         in_specs=[pl.BlockSpec(memory_space=pl.ANY)] * 2,
         out_specs=pl.BlockSpec(memory_space=pltpu.VMEM),
         scratch_shapes=[
             pltpu.VMEM((m, parts, total, 2 * cw), jnp.bfloat16),
             pltpu.VMEM((total + LAG, own), jnp.bfloat16),
-            pltpu.VMEM((total, 2 * own), jnp.bfloat16),
+            pltpu.VMEM((2, total, own), jnp.bfloat16),
             pltpu.VMEM((total + LAG, 128), jnp.int32),
             pltpu.VMEM((total, 128), jnp.bfloat16),
-            pltpu.VMEM((EXTRA, 2 * own), jnp.float32),
+            pltpu.VMEM((2, EXTRA, own), jnp.float32),
+            pltpu.VMEM((m, parts, 2, 2, *piece), jnp.float32),
             pltpu.VMEM((m, parts, 2, *piece), jnp.float32),
-            pltpu.VMEM((m, parts, *piece), jnp.float32),
-            pltpu.VMEM((m, parts, levels, *piece), jnp.float32),
+            pltpu.VMEM((m, parts, 2, levels, *piece), jnp.float32),
             sem((2 * parts + 2,)),
             sem((2,)),
             sem((2,)),
@@ -303,10 +310,10 @@
             sem((m, parts)),
             sem((parts,)),
             sem((m, parts, 2)),
-            sem((m, parts)),
-            sem((m, parts)),
-            sem((m, parts)),
-            sem((m, parts, levels)),
+            sem((m, parts, 2)),
+            sem((m, parts, 2)),
+            sem((m, parts, 2)),
+            sem((m, parts, 2, levels)),
         ],
         compiler_params=pltpu.CompilerParams(
             collective_id=0, has_side_effects=True, vmem_limit_bytes=58 * 2**20),

time: 169 us -> 159 us (0.941)
  Pallas kernels: 156 us -> 145 us
    pallas_call x1, Pallas kernels: 156 us -> 145 us  [shards(): pl.pallas_call(functools.partial(kernel, n, m, cw), out_shape=jax.ShapeDt...]
where the time goes in v3:
time: 159 us; the launch traced here: 156 us
  Pallas kernels  145 us (91%)
  local copies, waits for them, and re-layouts  6.09 us (4%)
  other arithmetic  4.22 us (3%)
    pallas_call x1, Pallas kernels, shards(): pl.pallas_call(functools.partial(kernel, n, m, cw), out_shape=jax.ShapeDt...  145 us

profile of v3, /device:TPU:26, one launch (start us, length us, event | category | flops | bytes accessed | tf_op | source)
XLA Modules:
  0.0 156.3 jit_solution(9931998448143709583)
XLA Ops:
  0.6 3.0 %broadcast_in_dim.2.ids_ref = s32[3584,128]{1,0:T(8,128)} broadcast(s32[3584]{0:T(1024)} %param.3), dimensions={0} | broadcast | bytes 1849344 | tf_op jit(solution)/shard_map/broadcast_in_dim | solution.py:286
  3.6 145.3 %shard_map.41 = f32[2,136,1024]{2,1,0:T(8,128)} custom-call(bf16[3584,512]{1,0:T(8,128)(2,1)} %x_ref.1, s32[3584,128]{1,0:T(8,128)} %broadcast_in_dim.2.ids_ref), custom_call_target="tpu_custom_call" | custom-call | flops 15032385536 | bytes 7340032 | tf_op jit(solution)/shard_map/pallas_call | solution.py:290
  148.9 1.2 slice.19
  150.1 2.0 %slice_divide_fusion = f32[2,128,1024]{2,1,0:T(8,128)S(1)} fusion(f32[2,136,1024]{2,1,0:T(8,128)} %shard_map.41, f32[]{:T(128)} %bitcast), kind=kLoop, calls=%fused_computation.1 | loop fusion | flops 262144 | bytes 2097156 | tf_op jit(solution)/shard_map/div | solution.py:328
  152.1 1.4 slice_divide_fusion.1
  153.5 0.9 slice.20
  154.4 0.7 dynamic-slice_divide_fusion
  155.1 0.2 bitcast_subtract_fusion
  155.2 1.0 fusion

commit v4 on v3

--- a/solution.py
+++ b/solution.py
@@ -214,7 +214,7 @@
         return carry
 
     def finished(p, k):
-        return jnp.maximum(k - 1 - p, 0)
+        return jnp.maximum(k - 1 - 2 * p, 0)
 
     def step(k, carry):
         for p in range(levels + 1):
@@ -258,7 +258,7 @@
                           functools.partial(stage, p), 0)
         return carry
 
-    lax.fori_loop(units, units + levels + 2, drain, 0)
+    lax.fori_loop(units, units + 2 * levels + 2, drain, 0)
     for j in range(parts):
         for h in range(2):
             out_ref[j, :, h * own:(h + 1) * own] = tb[group, j, h, side]

time: 159 us -> 152 us (0.956); the launches traced: 156 us -> 151 us
  Pallas kernels: 145 us -> 140 us
    pallas_call x1, Pallas kernels: 145 us -> 140 us  [shards(): pl.pallas_call(functools.partial(kernel, n, m, cw), out_shape=jax.ShapeDt...]
where the time goes in v4:
time: 152 us; the launch traced here: 151 us
  Pallas kernels  140 us (92%)
  local copies, waits for them, and re-layouts  6.09 us (4%)
  other arithmetic  4.22 us (3%)
    pallas_call x1, Pallas kernels, shards(): pl.pallas_call(functools.partial(kernel, n, m, cw), out_shape=jax.ShapeDt...  140 us

profile of v4, /device:TPU:26, one launch (start us, length us, event | category | flops | bytes accessed | tf_op | source)
XLA Modules:
  0.0 151.1 jit_solution(16926131055441264902)
XLA Ops:
  0.6 3.0 %broadcast_in_dim.2.ids_ref = s32[3584,128]{1,0:T(8,128)} broadcast(s32[3584]{0:T(1024)} %param.3), dimensions={0} | broadcast | bytes 1849344 | tf_op jit(solution)/shard_map/broadcast_in_dim | solution.py:286
  3.6 140.1 %shard_map.41 = f32[2,136,1024]{2,1,0:T(8,128)} custom-call(bf16[3584,512]{1,0:T(8,128)(2,1)} %x_ref.1, s32[3584,128]{1,0:T(8,128)} %broadcast_in_dim.2.ids_ref), custom_call_target="tpu_custom_call" | custom-call | flops 15032385536 | bytes 7340032 | tf_op jit(solution)/shard_map/pallas_call | solution.py:290
  143.7 1.2 slice.19
  144.9 2.0 %slice_divide_fusion = f32[2,128,1024]{2,1,0:T(8,128)S(1)} fusion(f32[2,136,1024]{2,1,0:T(8,128)} %shard_map.41, f32[]{:T(128)} %bitcast), kind=kLoop, calls=%fused_computation.1 | loop fusion | flops 262144 | bytes 2097156 | tf_op jit(solution)/shard_map/div | solution.py:328
  146.9 1.4 slice_divide_fusion.1
  148.3 0.9 slice.20
  149.2 0.7 dynamic-slice_divide_fusion
  149.8 0.2 bitcast_subtract_fusion
  150.0 1.0 fusion
